TPU v7x, 128 devices: a whole 4x4x4 slice. The times are simulated.
128 devices in a mesh: dp: 64 (over x_lo, z, y, core), tensor: 2 (over x_hi).
Axes of the slice: x: 4 (x_hi: 2, x_lo: 2; x = x_hi * 2 + x_lo), y: 4, z: 4, core: 2. Of those that a mesh axis runs over, the one named last changes fastest.
Arguments:
- tokens: bfloat16 [64, 512, 768], P('dp', 'tensor'), may hold values from -6 to 6
- doc_lengths: int32 [64, 2], P('dp'), may hold values from 0 to 512, as said below
- qkv_weight: bfloat16 [2, 3, 768, 768], P(None, None, 'tensor', 'dp'), may hold values from -0.21875 to 0.21875
- out_weight: bfloat16 [2, 768, 768], P(None, 'tensor', 'dp'), may hold values from -0.875 to 0.875
- inner_weight: bfloat16 [2, 3072, 768], P(None, 'tensor', 'dp'), may hold values from -0.21875 to 0.21875
- down_weight: bfloat16 [2, 3072, 768], P(None, 'tensor', 'dp'), may hold values from -0.109375 to 0.109375
- query_value_bias: float32 [2, 2, 768], P(None, None, 'tensor'), may hold values from -3 to 3
- hidden_bias: float32 [2, 3072], P(None, 'tensor'), may hold values from -3 to 3
- shifts: float32 [2, 4, 768], replicated, may hold values from -3 to 3
- gains: float32 [2, 2, 768], replicated, may hold values from 0.1 to 1.9
- cotangent: float32 [64, 512, 768], P('dp', 'tensor'), may hold values from -6 to 6
Outputs:
- output: float32 [64, 512, 768], P('dp', 'tensor')
- input_grad: float32 [64, 512, 768], P('dp', 'tensor')
- qkv_weight_grad: float32 [2, 3, 768, 768], P(None, None, 'tensor', 'dp')
- out_weight_grad: float32 [2, 768, 768], P(None, 'tensor', 'dp')
- inner_weight_grad: float32 [2, 3072, 768], P(None, 'tensor', 'dp')
- down_weight_grad: float32 [2, 3072, 768], P(None, 'tensor', 'dp')
- query_value_bias_grad: float32 [2, 2, 768], P(None, None, 'tensor')
- hidden_bias_grad: float32 [2, 3072], P(None, 'tensor')
- shift_grad: float32 [2, 4, 768], replicated
- gain_grad: float32 [2, 2, 768], replicated
Inputs may be any that keep to these rules, and one draw needn't show every extreme that they name: `doc_lengths`: each row holds a first document of more than 256 positions from its start, then a second one of 64 positions or more, or none, then padding; in every draw one row is a single document that fills it.
All inputs are finite; a program needn't handle non-finite values.
Results may differ from a plain program's by a relative error of at most 0.02.
Values may be sent and summed in bfloat16 or wider, within the bound.
No kernel may reach another device: no remote copies, remote signals or barrier semaphores. Data moves between devices by JAX's collectives and lax.ppermute only.
A program may use at most 192 MiB of HBM per device.

v0:
```python
import math

import jax
import jax.numpy as jnp
from jax import lax
from jax.sharding import PartitionSpec as P

HEAD = 64
LAYERS = 2


epsilon = 1e-06
masked_value = -1e30


def layer_norm(values, gain_vec, shift_vec):
    center = values - jnp.mean(values, axis=-1, keepdims=True)
    variance = jnp.mean(center * center, axis=-1, keepdims=True)
    return center * lax.rsqrt(variance + epsilon) * gain_vec + shift_vec


def exact_gelu(values):
    return jax.nn.gelu(values, approximate=False)


def contract_rows(left_op, right_op):
    return lax.dot_general(
        left_op, right_op, (((0,), (0,)), ((), ())), preferred_element_type=jnp.float32
    )


def contract_cols(left_op, right_op):
    return lax.dot_general(
        left_op, right_op, (((1,), (1,)), ((), ())), preferred_element_type=jnp.float32
    )


def plain_dot(left_op, right_op):
    return jnp.dot(left_op, right_op, preferred_element_type=jnp.float32)


def fetch_forward(qkv_weight, out_weight, inner_weight, down_weight, layer_idx):
    qkv_piece = qkv_weight[layer_idx].reshape(-1, qkv_weight.shape[3])
    return (
        lax.all_gather(qkv_piece, "dp", axis=1, tiled=True),
        lax.all_gather(out_weight[layer_idx], "dp", axis=1, tiled=True),
        lax.all_gather(inner_weight[layer_idx], "dp", axis=1, tiled=True),
        lax.all_gather(down_weight[layer_idx], "dp", axis=1, tiled=True),
    )


def fetch_backward(qkv_weight, out_weight, inner_weight, down_weight, layer_idx):
    qkv_piece = qkv_weight[layer_idx].reshape(-1, qkv_weight.shape[3])
    return (
        lax.all_gather(qkv_piece, "dp", axis=1, tiled=True),
        lax.all_gather(out_weight[layer_idx], "dp", axis=1, tiled=True),
        lax.all_gather(inner_weight[layer_idx], "dp", axis=1, tiled=True),
        lax.all_gather(down_weight[layer_idx], "dp", axis=1, tiled=True),
    )


def attention_scores(query_h, key_h, same_doc, scale_factor):
    scores = (
        jnp.einsum("rqhd,rkhd->rhqk", query_h, key_h, preferred_element_type=jnp.float32)
        * scale_factor
    )
    return jnp.where(same_doc[:, None], scores, masked_value)


def body(
    tokens,
    doc_lengths,
    qkv_weight,
    out_weight,
    inner_weight,
    down_weight,
    query_value_bias,
    hidden_bias,
    shifts,
    gains,
    cotangent,
):
    row_count, half_len, features = tokens.shape
    seq_len = half_len * lax.axis_size("tensor")
    head_cols = qkv_weight.shape[2]
    local_heads = head_cols // HEAD
    scale_factor = 1.0 / math.sqrt(HEAD)
    flat_rows = row_count * seq_len
    position = jnp.arange(seq_len, dtype=jnp.int32)[None, :]
    first_end = doc_lengths[:, 0:1]
    second_end = first_end + doc_lengths[:, 1:2]
    segment = (position >= first_end).astype(jnp.int32) + (position >= second_end).astype(jnp.int32)
    same_doc = segment[:, :, None] == segment[:, None, :]
    hidden_state = tokens.astype(jnp.float32)
    saved_acts = []
    for layer_idx in range(LAYERS):
        qkv_full, out_full, inner_full, down_full = fetch_forward(
            qkv_weight, out_weight, inner_weight, down_weight, layer_idx
        )
        state_low = hidden_state.astype(jnp.bfloat16)
        rows_flat = lax.all_gather(state_low, "tensor", axis=1, tiled=True).reshape(
            flat_rows, features
        )
        projected = contract_cols(rows_flat, qkv_full).reshape(flat_rows, 3, head_cols)
        query_b = (projected[:, 0] + query_value_bias[layer_idx, 0]).astype(jnp.bfloat16)
        key_b = projected[:, 1].astype(jnp.bfloat16)
        value_b = (projected[:, 2] + query_value_bias[layer_idx, 1]).astype(jnp.bfloat16)
        query_h = query_b.reshape(row_count, seq_len, local_heads, HEAD)
        key_h = key_b.reshape(row_count, seq_len, local_heads, HEAD)
        value_h = value_b.reshape(row_count, seq_len, local_heads, HEAD)
        scores = attention_scores(query_h, key_h, same_doc, scale_factor)
        row_max = jnp.max(scores, axis=-1, keepdims=True)
        raised = jnp.exp(scores - row_max)
        row_total = jnp.sum(raised, axis=-1, keepdims=True)
        attn_probs = (raised / row_total).astype(jnp.bfloat16)
        log_total = row_max + jnp.log(row_total)
        attended = jnp.einsum(
            "rhqk,rkhd->rqhd", attn_probs, value_h, preferred_element_type=jnp.float32
        )
        attended_b = attended.reshape(flat_rows, head_cols).astype(jnp.bfloat16)
        attn_part = plain_dot(attended_b, out_full).reshape(row_count, seq_len, features)
        branch = lax.psum_scatter(
            attn_part.astype(jnp.bfloat16), "tensor", scatter_dimension=1, tiled=True
        ).astype(jnp.float32)
        normed, norm_first_back = jax.vjp(
            layer_norm,
            hidden_state + branch + shifts[layer_idx, 0],
            gains[layer_idx, 0],
            shifts[layer_idx, 1],
        )
        normed_low = normed.astype(jnp.bfloat16)
        normed_flat = lax.all_gather(normed_low, "tensor", axis=1, tiled=True).reshape(
            flat_rows, features
        )
        pre_act = contract_cols(normed_flat, inner_full) + hidden_bias[layer_idx]
        activated, gelu_back = jax.vjp(exact_gelu, pre_act)
        activated_b = activated.astype(jnp.bfloat16)
        mlp_part = plain_dot(activated_b, down_full).reshape(row_count, seq_len, features)
        mlp_out = lax.psum_scatter(
            mlp_part.astype(jnp.bfloat16), "tensor", scatter_dimension=1, tiled=True
        ).astype(jnp.float32)
        hidden_state, norm_second_back = jax.vjp(
            layer_norm,
            normed + mlp_out + shifts[layer_idx, 2],
            gains[layer_idx, 1],
            shifts[layer_idx, 3],
        )
        held_weights = None
        saved_acts.append(
            (
                held_weights,
                rows_flat,
                query_h,
                key_h,
                value_h,
                log_total,
                attended_b,
                normed_flat,
                gelu_back,
                activated_b,
                norm_first_back,
                norm_second_back,
            )
        )
    state_grad = cotangent
    weight_parts = [None] * LAYERS
    shift_parts = [None] * LAYERS
    gain_parts = [None] * LAYERS
    qv_parts = [None] * LAYERS
    hidden_parts = [None] * LAYERS
    for layer_idx in reversed(range(LAYERS)):
        (
            held_weights,
            rows_flat,
            query_h,
            key_h,
            value_h,
            log_total,
            attended_b,
            normed_flat,
            gelu_back,
            activated_b,
            norm_first_back,
            norm_second_back,
        ) = saved_acts[layer_idx]
        qkv_full, out_full, inner_full, down_full = fetch_backward(
            qkv_weight, out_weight, inner_weight, down_weight, layer_idx
        )
        pre_two_grad, gain_two_grad, beta_two_grad = norm_second_back(state_grad)
        mlp_grad_b = pre_two_grad.astype(jnp.bfloat16)
        mlp_grad_full = lax.all_gather(mlp_grad_b, "tensor", axis=1, tiled=True).reshape(
            flat_rows, features
        )
        down_local = contract_rows(activated_b, mlp_grad_full)
        activated_grad = contract_cols(mlp_grad_full, down_full)
        pre_act_grad = gelu_back(activated_grad)[0].astype(jnp.bfloat16)
        hidden_bias_part = jnp.sum(pre_act_grad.astype(jnp.float32), axis=0)
        inner_local = contract_rows(pre_act_grad, normed_flat)
        normed_part = plain_dot(pre_act_grad, inner_full).reshape(row_count, seq_len, features)
        normed_grad = pre_two_grad + lax.psum_scatter(
            normed_part.astype(jnp.bfloat16), "tensor", scatter_dimension=1, tiled=True
        ).astype(jnp.float32)
        pre_one_grad, gain_one_grad, beta_one_grad = norm_first_back(normed_grad)
        attn_grad_b = pre_one_grad.astype(jnp.bfloat16)
        attn_grad_full = lax.all_gather(attn_grad_b, "tensor", axis=1, tiled=True).reshape(
            flat_rows, features
        )
        out_local = contract_rows(attended_b, attn_grad_full)
        attended_grad = contract_cols(attn_grad_full, out_full).astype(jnp.bfloat16)
        attended_grad_h = attended_grad.reshape(row_count, seq_len, local_heads, HEAD)
        scores = attention_scores(query_h, key_h, same_doc, scale_factor)
        probs_full = jnp.exp(scores - log_total)
        probs_low = probs_full.astype(jnp.bfloat16)
        value_grad = jnp.einsum(
            "rhqk,rqhd->rkhd", probs_low, attended_grad_h, preferred_element_type=jnp.float32
        )
        prob_grad = jnp.einsum(
            "rqhd,rkhd->rhqk", attended_grad_h, value_h, preferred_element_type=jnp.float32
        )
        row_dot = jnp.sum(prob_grad * probs_full, axis=-1, keepdims=True)
        score_grad = (probs_full * (prob_grad - row_dot)).astype(jnp.bfloat16)
        query_grad = (
            jnp.einsum("rhqk,rkhd->rqhd", score_grad, key_h, preferred_element_type=jnp.float32)
            * scale_factor
        )
        key_grad = (
            jnp.einsum("rhqk,rqhd->rkhd", score_grad, query_h, preferred_element_type=jnp.float32)
            * scale_factor
        )
        query_grad_b = query_grad.reshape(flat_rows, head_cols).astype(jnp.bfloat16)
        key_grad_b = key_grad.reshape(flat_rows, head_cols).astype(jnp.bfloat16)
        value_grad_b = value_grad.reshape(flat_rows, head_cols).astype(jnp.bfloat16)
        qv_parts[layer_idx] = jnp.stack(
            [
                jnp.sum(query_grad_b.astype(jnp.float32), axis=0),
                jnp.sum(value_grad_b.astype(jnp.float32), axis=0),
            ]
        )
        qkv_grads_b = jnp.concatenate([query_grad_b, key_grad_b, value_grad_b], axis=1)
        qkv_local = contract_rows(qkv_grads_b, rows_flat)
        rows_part = plain_dot(qkv_grads_b, qkv_full).reshape(row_count, seq_len, features)
        state_grad = pre_one_grad + lax.psum_scatter(
            rows_part.astype(jnp.bfloat16), "tensor", scatter_dimension=1, tiled=True
        ).astype(jnp.float32)
        shift_parts[layer_idx] = jnp.stack(
            [
                jnp.sum(pre_one_grad, axis=(0, 1)),
                beta_one_grad,
                jnp.sum(pre_two_grad, axis=(0, 1)),
                beta_two_grad,
            ]
        )
        gain_parts[layer_idx] = jnp.stack([gain_one_grad, gain_two_grad])
        hidden_parts[layer_idx] = hidden_bias_part
        weight_parts[layer_idx] = (
            lax.psum_scatter(qkv_local, "dp", scatter_dimension=1, tiled=True),
            lax.psum_scatter(out_local, "dp", scatter_dimension=1, tiled=True),
            lax.psum_scatter(inner_local, "dp", scatter_dimension=1, tiled=True),
            lax.psum_scatter(down_local, "dp", scatter_dimension=1, tiled=True),
        )
    qkv_stack = jnp.stack([parts[0] for parts in weight_parts])
    out_stack = jnp.stack([parts[1] for parts in weight_parts])
    inner_stack = jnp.stack([parts[2] for parts in weight_parts])
    down_stack = jnp.stack([parts[3] for parts in weight_parts])
    qkv_result = qkv_stack.reshape(LAYERS, 3, head_cols, -1)
    shift_total, gain_total = lax.psum(
        (jnp.stack(shift_parts), jnp.stack(gain_parts)), ("dp", "tensor")
    )
    qv_total, hidden_total = lax.psum((jnp.stack(qv_parts), jnp.stack(hidden_parts)), "dp")
    return (
        hidden_state,
        state_grad,
        qkv_result,
        out_stack,
        inner_stack,
        down_stack,
        qv_total,
        hidden_total,
        shift_total,
        gain_total,
    )


def solution(mesh):
    in_specs = (
        P("dp", "tensor", None),
        P("dp", None),
        P(None, None, "tensor", "dp"),
        P(None, "tensor", "dp"),
        P(None, "tensor", "dp"),
        P(None, "tensor", "dp"),
        P(None, None, "tensor"),
        P(None, "tensor"),
        P(),
        P(),
        P("dp", "tensor", None),
    )
    out_specs = (
        P("dp", "tensor", None),
        P("dp", "tensor", None),
        P(None, None, "tensor", "dp"),
        P(None, "tensor", "dp"),
        P(None, "tensor", "dp"),
        P(None, "tensor", "dp"),
        P(None, None, "tensor"),
        P(None, "tensor"),
        P(),
        P(),
    )
    return jax.shard_map(body, mesh=mesh, in_specs=in_specs, out_specs=out_specs, check_vma=False)
```

profile of v0, /device:TPU:1, one launch (start us, length us, event | category | flops | bytes accessed | tf_op | source)
XLA Modules:
  0.0 2011.0 jit_solution(12341034015533155001)
XLA Ops:
  14.4 88.4 %all-gather = bf16[1,384,768]{1,0,2:T(2,128)(2,1)S(1)} all-gather(bf16[1,384,12]{1,0,2:T(2,128)(2,1)S(1)} %get-tuple-element.125), channel_id=2, replica_groups=mesh['dp'=64,'tensor'=2] {'dp'}, dimensions={2}, use_global_device_ids=true | all-gather | bytes 599040 | tf_op jit(solution)/shard_map/all_gather | solution.py:46
  107.2 13.2 all_gather.56
  141.4 85.6 %all-gather.15.cloned.1.call-done = bf16[1,1536,768]{1,0,2:T(2,128)(2,1)} async-done(((bf16[1,1536,12]{1,0,2:T(2,128)(2,1)}), bf16[1,1536,768]{1,0,2:T(2,128)(2,1)}) %all-gather.15.cloned.1.call-update) | async-done | bytes 2359312 | tf_op jit(solution)/shard_map/all_gather | solution.py:47
  238.8 96.3 %all-gather.17.cloned.1.call-done = bf16[1,1536,768]{1,0,2:T(2,128)(2,1)} async-done(((bf16[1,1536,12]{1,0,2:T(2,128)(2,1)}), bf16[1,1536,768]{1,0,2:T(2,128)(2,1)}) %all-gather.17.cloned.1.call-update) | async-done | bytes 2359312 | tf_op jit(solution)/shard_map/all_gather | solution.py:48
  335.1 11.7 copy.61
  361.8 12.9 all_gather.59
  390.3 86.4 %all-gather.3 = bf16[1,384,768]{1,0,2:T(2,128)(2,1)S(1)} all-gather(bf16[1,384,12]{1,0,2:T(2,128)(2,1)S(1)} %get-tuple-element.124), channel_id=5, replica_groups=mesh['dp'=64,'tensor'=2] {'dp'}, dimensions={2}, use_global_device_ids=true | all-gather | bytes 599040 | tf_op jit(solution)/shard_map/all_gather | solution.py:46
  489.5 12.2 all_gather.62
  511.3 85.4 %all-gather.19.cloned.1.call-done = bf16[1,1536,768]{1,0,2:T(2,128)(2,1)} async-done(((bf16[1,1536,12]{1,0,2:T(2,128)(2,1)}), bf16[1,1536,768]{1,0,2:T(2,128)(2,1)}) %all-gather.19.cloned.1.call-update) | async-done | bytes 2359312 | tf_op jit(solution)/shard_map/all_gather | solution.py:47
  596.7 11.7 copy.66
  608.4 96.9 %all-gather.21.cloned.1.call-done = bf16[1,1536,768]{1,0,2:T(2,128)(2,1)} async-done(((bf16[1,1536,12]{1,0,2:T(2,128)(2,1)}), bf16[1,1536,768]{1,0,2:T(2,128)(2,1)}) %all-gather.21.cloned.1.call-update) | async-done | bytes 2359312 | tf_op jit(solution)/shard_map/all_gather | solution.py:48
  705.3 11.7 copy.67
  730.8 12.7 all_gather.65
  756.8 21.9 %reduce-scatter.31.cloned.1.call-done = bf16[1,256,768]{2,1,0:T(8,128)(2,1)} async-done(((bf16[1,512,768]{2,1,0:T(8,128)(2,1)}), bf16[1,256,768]{2,1,0:T(8,128)(2,1)}) %reduce-scatter.31.cloned.1.call-update) | async-done | bytes 393232 | tf_op jit(solution)/shard_map/reduce_scatter | solution.py:139
  782.8 12.3 all_gather.68
  802.2 21.2 %reduce-scatter.33.cloned.1.call-done = bf16[1,256,768]{2,1,0:T(8,128)(2,1)} async-done(((bf16[1,512,768]{2,1,0:T(8,128)(2,1)}), bf16[1,256,768]{2,1,0:T(8,128)(2,1)}) %reduce-scatter.33.cloned.1.call-update) | async-done | bytes 393232 | tf_op jit(solution)/shard_map/reduce_scatter | solution.py:200
  828.2 12.3 all_gather.69
  860.0 16.7 reduce-scatter.35.cloned.1.call-done
  880.6 12.4 all_gather.70
  928.2 12.6 all_gather.71
  957.4 212.7 %fusion.138 = (f32[1152,16]{0,1:T(8,128)S(1)}, f32[1152,16]{0,1:T(8,128)S(1)}, f32[384,16]{0,1:T(8,128)S(1)}, f32[384,16]{0,1:T(8,128)S(1)}, f32[1536,16]{0,1:T(...) fusion(f32[1152,768]{0,1:T(8,128)} %fusion.107, f32[1152,768]{0,1:T(8,128)} %fusion.114, ...), kind=kCustom, calls=%all-reduce-scatter.8 | all-reduce-scatter fusion | flops 9437185 | bytes 28901888
  1355.1 269.1 %all-reduce.17 = (f32[2,2,384]{2,1,0:T(2,128)}, f32[2,1536]{1,0:T(2,128)}) all-reduce(f32[2,2,384]{2,1,0:T(2,128)S(1)} %pad_maximum_fusion.13, f32[2,1536]{1,0:T(2,128)S(1)} %pad_maximum_fusion.11), channel_id=1, replica_groups=mesh['dp'=64,'tensor'=2] {'dp'}, use_global_device_ids=true, to_apply=%region_42.43 | all-reduce | flops 4608 | bytes 36864 | tf_op jit(solution)/shard_map/psum | solution.py:269
  1632.7 12.6 collective-permute-start.100
  1683.9 69.4 %all-reduce.16 = (f32[2,4,768]{2,1,0:T(4,128)}, f32[2,2,768]{2,1,0:T(2,128)}) all-reduce(f32[2,4,768]{2,1,0:T(4,128)S(1)} %pad_maximum_fusion.10, f32[2,2,768]{2,1,0:T(2,128)S(1)} %pad_maximum_fusion.12), channel_id=1, replica_groups=mesh['dp'=64,'tensor'=2] {'dp','tensor'}, use_global_device_ids=true, to_apply=%region_54.55 | all-reduce | flops 9216 | bytes 73728 | tf_op jit(solution)/shard_map/psum | solution.py:266
  1753.4 13.1 concatenate.11
  1766.6 13.1 concatenate.12
  1827.1 15.5 concatenate.9
  1858.0 15.6 concatenate.10
  1895.9 13.4 concatenate.15
  1924.1 14.2 concatenate.16
  1960.1 14.2 concatenate.13
  1974.5 26.0 %concatenate.14 = f32[1536,268]{0,1:T(8,128)} concatenate(f32[1536,12]{0,1:T(8,128)S(1)} %copy-done.79, f32[1536,16]{0,1:T(8,128)} %collective-permute-done.94, f32[1536,16]{0,1:T(8,128)} %collective-permute-done.93, f32[1536,16]{0,1:T(8,128)} %collective-permute-done.92, f32[1536,16]{0,1:T(8,128)} %collective-permute-done.91, f32[1536,16]{0,1:T(8,128)} %collective-permute-done.90, ...), dimensions={1} | concatenate | bytes 3293184
  (914 shorter events, 567.4 us)
Async XLA Ops:
  7.2 113.5 %all-gather.23.cloned.1.call-start = ((), (), s32[]{:S(2)}) async-start(), calls=%async_computation.20 | async-start | bytes 2396160 | tf_op jit(solution)/shard_map/all_gather | solution.py:45
  9.0 218.1 %all-gather.15.cloned.1.call-start = ((), (), s32[]{:S(2)}) async-start(), calls=%async_computation.16 | async-start | bytes 4792320 | tf_op jit(solution)/shard_map/all_gather | solution.py:47
  10.8 324.3 %all-gather.17.cloned.1.call-start = ((), (), s32[]{:S(2)}) async-start(), calls=%async_computation.17 | async-start | bytes 4792320 | tf_op jit(solution)/shard_map/all_gather | solution.py:48
  12.6 345.3 %reduce-scatter.25.cloned.1.call-start = ((), (), s32[]{:S(2)}) async-start(), calls=%async_computation.8 | async-start | bytes 1179648 | tf_op jit(solution)/shard_map/reduce_scatter | solution.py:122
  138.7 340.9 %all-gather.25.cloned.1.call-start = ((), (), s32[]{:S(2)}) async-start(), calls=%async_computation.21 | async-start | bytes 2396160 | tf_op jit(solution)/shard_map/all_gather | solution.py:45
  139.5 347.9 %reduce-scatter.27.cloned.1.call-start = ((), (), s32[]{:S(2)}) async-start(), calls=%async_computation.9 | async-start | bytes 1179648 | tf_op jit(solution)/shard_map/reduce_scatter | solution.py:139
  388.0 208.7 %all-gather.19.cloned.1.call-start = ((), (), s32[]{:S(2)}) async-start(), calls=%async_computation.18 | async-start | bytes 4792320 | tf_op jit(solution)/shard_map/all_gather | solution.py:47
  388.7 316.5 %all-gather.21.cloned.1.call-start = ((), (), s32[]{:S(2)}) async-start(), calls=%async_computation.19 | async-start | bytes 4792320 | tf_op jit(solution)/shard_map/all_gather | solution.py:48
  389.5 338.7 %reduce-scatter.29.cloned.1.call-start = ((), (), s32[]{:S(2)}) async-start(), calls=%async_computation.10 | async-start | bytes 1179648 | tf_op jit(solution)/shard_map/reduce_scatter | solution.py:122
  511.3 267.4 %reduce-scatter.31.cloned.1.call-start = ((), (), s32[]{:S(2)}) async-start(), calls=%async_computation.11 | async-start | bytes 1179648 | tf_op jit(solution)/shard_map/reduce_scatter | solution.py:139
  756.8 66.6 %reduce-scatter.33.cloned.1.call-start = ((), (), s32[]{:S(2)}) async-start(), calls=%async_computation.12 | async-start | bytes 1179648 | tf_op jit(solution)/shard_map/reduce_scatter | solution.py:200
  801.4 75.3 %reduce-scatter.35.cloned.1.call-start = ((), (), s32[]{:S(2)}) async-start(), calls=%async_computation.13 | async-start | bytes 1179648 | tf_op jit(solution)/shard_map/reduce_scatter | solution.py:242
  854.8 68.8 %reduce-scatter.37.cloned.1.call-start = ((), (), s32[]{:S(2)}) async-start(), calls=%async_computation.14 | async-start | bytes 1179648 | tf_op jit(solution)/shard_map/reduce_scatter | solution.py:200
  901.7 1100.6 %reduce-scatter.39.cloned.1.call-start = ((), (), s32[]{:S(2)}) async-start(), calls=%async_computation.15 | async-start | bytes 1179648 | tf_op jit(solution)/shard_map/reduce_scatter | solution.py:242
  1170.1 28.9 %collective-permute-start.32 = (f32[384,16]{0,1:T(8,128)S(1)}, f32[384,16]{0,1:T(8,128)S(1)}, u32[]{:S(2)}, u32[]{:S(2)}) collective-permute-start(f32[384,16]{0,1:T(8,128)S(1)} %get-tuple-element.88), channel_id=1, source_target_pairs={{0,2},{2,4},{4,6},{6,8},{8,10},{10,12},{12,14},{14,16},{16,18},{18... | collective-permute-start | bytes 73736
  1346.6 277.6 %collective-permute-start.21 = (f32[1152,16]{0,1:T(8,128)S(1)}, f32[1152,16]{0,1:T(8,128)S(1)}, u32[]{:S(2)}, u32[]{:S(2)}) collective-permute-start(f32[1152,16]{0,1:T(8,128)S(1)} %get-tuple-element.85), channel_id=1, source_target_pairs={{0,12},{2,14},{4,16},{6,18},{8,20},{10,22},{12,24},{14,26},{16,28}... | collective-permute-start | bytes 221192
  1348.1 277.4 %collective-permute-start.22 = (f32[1152,16]{0,1:T(8,128)S(1)}, f32[1152,16]{0,1:T(8,128)S(1)}, u32[]{:S(2)}, u32[]{:S(2)}) collective-permute-start(f32[1152,16]{0,1:T(8,128)S(1)} %get-tuple-element.85), channel_id=1, source_target_pairs={{0,14},{2,16},{4,18},{6,20},{8,22},{10,24},{12,26},{14,28},{16,30}... | collective-permute-start | bytes 221192
  1349.7 277.1 %collective-permute-start.23 = (f32[1152,16]{0,1:T(8,128)S(1)}, f32[1152,16]{0,1:T(8,128)S(1)}, u32[]{:S(2)}, u32[]{:S(2)}) collective-permute-start(f32[1152,16]{0,1:T(8,128)S(1)} %get-tuple-element.85), channel_id=1, source_target_pairs={{0,16},{2,18},{4,20},{6,22},{8,24},{10,26},{12,28},{14,30},{16,32}... | collective-permute-start | bytes 221192
  1351.1 277.7 %collective-permute-start.24 = (f32[1152,16]{0,1:T(8,128)S(1)}, f32[1152,16]{0,1:T(8,128)S(1)}, u32[]{:S(2)}, u32[]{:S(2)}) collective-permute-start(f32[1152,16]{0,1:T(8,128)S(1)} %get-tuple-element.85), channel_id=1, source_target_pairs={{0,18},{2,20},{4,22},{6,24},{8,26},{10,28},{12,30},{14,32},{16,34}... | collective-permute-start | bytes 221192
  1352.8 277.9 %collective-permute-start.25 = (f32[1152,16]{0,1:T(8,128)S(1)}, f32[1152,16]{0,1:T(8,128)S(1)}, u32[]{:S(2)}, u32[]{:S(2)}) collective-permute-start(f32[1152,16]{0,1:T(8,128)S(1)} %get-tuple-element.85), channel_id=1, source_target_pairs={{0,20},{2,22},{4,24},{6,26},{8,28},{10,30},{12,32},{14,34},{16,36}... | collective-permute-start | bytes 221192
  1671.1 108.6 %collective-permute-start.110 = (f32[1536,16]{0,1:T(8,128)S(1)}, f32[1536,16]{0,1:T(8,128)S(1)}, u32[]{:S(2)}, u32[]{:S(2)}) collective-permute-start(f32[1536,16]{0,1:T(8,128)S(1)} %get-tuple-element.92), channel_id=1, source_target_pairs={{0,30},{2,32},{4,34},{6,36},{8,38},{10,40},{12,42},{14,44},{16,46}... | collective-permute-start | bytes 294920
  1672.7 109.4 %collective-permute-start.96 = (f32[1536,16]{0,1:T(8,128)S(1)}, f32[1536,16]{0,1:T(8,128)S(1)}, u32[]{:S(2)}, u32[]{:S(2)}) collective-permute-start(f32[1536,16]{0,1:T(8,128)S(1)} %get-tuple-element.92), channel_id=1, source_target_pairs={{0,2},{2,4},{4,6},{6,8},{8,10},{10,12},{12,14},{14,16},{16,18},{18... | collective-permute-start | bytes 294920
  1675.5 111.0 %collective-permute-start.97 = (f32[1536,16]{0,1:T(8,128)S(1)}, f32[1536,16]{0,1:T(8,128)S(1)}, u32[]{:S(2)}, u32[]{:S(2)}) collective-permute-start(f32[1536,16]{0,1:T(8,128)S(1)} %get-tuple-element.92), channel_id=1, source_target_pairs={{0,4},{2,6},{4,8},{6,10},{8,12},{10,14},{12,16},{14,18},{16,20},{1... | collective-permute-start | bytes 294920
  1680.1 108.7 %collective-permute-start.98 = (f32[1536,16]{0,1:T(8,128)S(1)}, f32[1536,16]{0,1:T(8,128)S(1)}, u32[]{:S(2)}, u32[]{:S(2)}) collective-permute-start(f32[1536,16]{0,1:T(8,128)S(1)} %get-tuple-element.92), channel_id=1, source_target_pairs={{0,6},{2,8},{4,10},{6,12},{8,14},{10,16},{12,18},{14,20},{16,22},{... | collective-permute-start | bytes 294920
  1681.4 110.1 %collective-permute-start.99 = (f32[1536,16]{0,1:T(8,128)S(1)}, f32[1536,16]{0,1:T(8,128)S(1)}, u32[]{:S(2)}, u32[]{:S(2)}) collective-permute-start(f32[1536,16]{0,1:T(8,128)S(1)} %get-tuple-element.92), channel_id=1, source_target_pairs={{0,8},{2,10},{4,12},{6,14},{8,16},{10,18},{12,20},{14,22},{16,24},... | collective-permute-start | bytes 294920
  1816.7 29.3 %collective-permute-start.123 = (f32[1536,16]{0,1:T(8,128)S(1)}, f32[1536,16]{0,1:T(8,128)}, u32[]{:S(2)}, u32[]{:S(2)}) collective-permute-start(f32[1536,16]{0,1:T(8,128)S(1)} %get-tuple-element.91), channel_id=1, source_target_pairs={{0,24},{2,26},{4,28},{6,30},{8,32},{10,34},{12,36},{14,38},{16,40}... | collective-permute-start | bytes 294920
  1820.2 29.3 %collective-permute-start.124 = (f32[1536,16]{0,1:T(8,128)S(1)}, f32[1536,16]{0,1:T(8,128)}, u32[]{:S(2)}, u32[]{:S(2)}) collective-permute-start(f32[1536,16]{0,1:T(8,128)S(1)} %get-tuple-element.91), channel_id=1, source_target_pairs={{0,26},{2,28},{4,30},{6,32},{8,34},{10,36},{12,38},{14,40},{16,42}... | collective-permute-start | bytes 294920
  1822.1 31.1 %collective-permute-start.125 = (f32[1536,16]{0,1:T(8,128)S(1)}, f32[1536,16]{0,1:T(8,128)}, u32[]{:S(2)}, u32[]{:S(2)}) collective-permute-start(f32[1536,16]{0,1:T(8,128)S(1)} %get-tuple-element.91), channel_id=1, source_target_pairs={{0,28},{2,30},{4,32},{6,34},{8,36},{10,38},{12,40},{14,42},{16,44}... | collective-permute-start | bytes 294920
  1824.2 31.0 %collective-permute-start.126 = (f32[1536,16]{0,1:T(8,128)S(1)}, f32[1536,16]{0,1:T(8,128)}, u32[]{:S(2)}, u32[]{:S(2)}) collective-permute-start(f32[1536,16]{0,1:T(8,128)S(1)} %get-tuple-element.91), channel_id=1, source_target_pairs={{0,30},{2,32},{4,34},{6,36},{8,38},{10,40},{12,42},{14,44},{16,46}... | collective-permute-start | bytes 294920
  1842.7 30.9 %collective-permute-start.64 = (f32[1536,16]{0,1:T(8,128)S(1)}, f32[1536,16]{0,1:T(8,128)}, u32[]{:S(2)}, u32[]{:S(2)}) collective-permute-start(f32[1536,16]{0,1:T(8,128)S(1)} %get-tuple-element.90), channel_id=1, source_target_pairs={{0,2},{2,4},{4,6},{6,8},{8,10},{10,12},{12,14},{14,16},{16,18},{18... | collective-permute-start | bytes 294920
  1846.0 28.8 %collective-permute-start.65 = (f32[1536,16]{0,1:T(8,128)S(1)}, f32[1536,16]{0,1:T(8,128)}, u32[]{:S(2)}, u32[]{:S(2)}) collective-permute-start(f32[1536,16]{0,1:T(8,128)S(1)} %get-tuple-element.90), channel_id=1, source_target_pairs={{0,4},{2,6},{4,8},{6,10},{8,12},{10,14},{12,16},{14,18},{16,20},{1... | collective-permute-start | bytes 294920
  1909.3 29.0 %collective-permute-start.80 = (f32[1536,16]{0,1:T(8,128)S(1)}, f32[1536,16]{0,1:T(8,128)S(1)}, u32[]{:S(2)}, u32[]{:S(2)}) collective-permute-start(f32[1536,16]{0,1:T(8,128)S(1)} %get-tuple-element.89), channel_id=1, source_target_pairs={{0,2},{2,4},{4,6},{6,8},{8,10},{10,12},{12,14},{14,16},{16,18},{18... | collective-permute-start | bytes 294920
  (337 other events, 11483.5 us)
Sparse Core Ops, SparseCore 0:
  10.3 108.3 all-gather.22
  121.0 106.0 all-gather.14
  228.8 106.2 all-gather.16
  337.8 19.9 reduce-scatter.24
  360.1 104.1 all-gather.24
  467.3 20.0 reduce-scatter.26
  489.6 107.0 all-gather.18
  599.0 106.2 all-gather.20
  708.2 19.9 reduce-scatter.28
  756.9 21.7 reduce-scatter.30
  801.6 21.8 reduce-scatter.32
  855.0 21.7 reduce-scatter.34
  901.8 21.7 reduce-scatter.36
  1332.5 16.9 reduce-scatter.38
where the time goes:
time: 2030 us; the launch traced here: 2010 us
  blocking collectives  826 us (41%)
  waiting for transfers between devices  454 us (22%)
  starting transfers between devices  334 us (16%)
  local copies, waits for them, and re-layouts  236 us (12%)
  matrix products  98.7 us (5%)
  other arithmetic  41.5 us (2%)
  between operations  20.3 us (1%)
    unnamed x128, starting transfers between devices  333 us
    psum x1, blocking collectives, body(): lax.psum((jnp.stack(qv_parts), jnp.stack(hidden_parts)), 'dp')  269 us
    unnamed x1, blocking collectives  213 us
    all_gather x2, waiting for transfers between devices, fetch_forward(): lax.all_gather(down_weight[layer_idx], 'dp', axis=1, tiled=True)  193 us
    all_gather x2, blocking collectives, fetch_forward(): lax.all_gather(out_weight[layer_idx], 'dp', axis=1, tiled=True)  175 us
    all_gather x2, waiting for transfers between devices, fetch_forward(): lax.all_gather(inner_weight[layer_idx], 'dp', axis=1, tiled=True)  171 us
    unnamed x486, local copies, waits for them, and re-layouts  161 us
    psum x1, blocking collectives, body(): lax.psum((jnp.stack(shift_parts), jnp.stack(gain_parts)), ('dp', 'tensor'))  69.4 us
  transfers between devices with their start and end apart: 142, of which 11 were waited for; matrix products, arithmetic and copies ran while one was open for 14% of the time, Pallas kernels for 0%

commit v1 on v0

v1 whole, which is shorter than its diff:
```python
import math

import jax
import jax.numpy as jnp
from jax import lax
from jax.sharding import PartitionSpec as P

HEAD = 64
LAYERS = 2
ALL = ("tensor", "dp")


epsilon = 1e-06
masked_value = -1e30


def layer_norm(values, gain_vec, shift_vec):
    center = values - jnp.mean(values, axis=-1, keepdims=True)
    variance = jnp.mean(center * center, axis=-1, keepdims=True)
    inverse = lax.rsqrt(variance + epsilon)
    normal = center * inverse
    return normal * gain_vec + shift_vec, normal, inverse


def norm_back(grad, normal, inverse, gain_vec):
    scaled = grad * gain_vec
    mean_one = jnp.mean(scaled, axis=-1, keepdims=True)
    mean_two = jnp.mean(scaled * normal, axis=-1, keepdims=True)
    return inverse * (scaled - mean_one - normal * mean_two)


def exact_gelu(values):
    return jax.nn.gelu(values, approximate=False)


def nn(left, right):
    return lax.dot_general(left, right, (((1,), (0,)), ((), ())), preferred_element_type=jnp.float32)


def nt(left, right):
    return lax.dot_general(left, right, (((1,), (1,)), ((), ())), preferred_element_type=jnp.float32)


def tn(left, right):
    return lax.dot_general(left, right, (((0,), (0,)), ((), ())), preferred_element_type=jnp.float32)


def swap_halves(values):
    return lax.ppermute(values, "tensor", [(0, 1), (1, 0)])


def gather_weights(qkv_weight, out_weight, inner_weight, down_weight):
    layers = qkv_weight.shape[0]
    thin = qkv_weight.shape[3]
    piece = jnp.concatenate(
        [qkv_weight.reshape(layers, -1, thin), out_weight, inner_weight, down_weight], axis=1
    )
    width = piece.shape[1]
    piece = piece.transpose(0, 2, 1).reshape(layers * thin, width)
    whole = lax.all_gather(piece, ALL, axis=0, tiled=True)
    whole = whole.reshape(2, -1, layers, thin, width)
    return [whole[:, :, layer].reshape(2, -1, width) for layer in range(layers)]


def split_heads(matrix):
    return matrix.reshape(matrix.shape[0], -1, HEAD).transpose(1, 0, 2)


def join_heads(matrix):
    return matrix.transpose(1, 0, 2).reshape(matrix.shape[1], -1)


def body(
    tokens,
    doc_lengths,
    qkv_weight,
    out_weight,
    inner_weight,
    down_weight,
    query_value_bias,
    hidden_bias,
    shifts,
    gains,
    cotangent,
):
    half_len, features = tokens.shape[1:]
    thin = qkv_weight.shape[3]
    head_cols = qkv_weight.shape[2]
    hidden_cols = inner_weight.shape[1]
    scale_factor = 1.0 / math.sqrt(HEAD)
    tensor_idx = lax.axis_index("tensor")
    dp_idx = lax.axis_index("dp")

    weights = gather_weights(qkv_weight, out_weight, inner_weight, down_weight)
    bias_rows = jnp.concatenate(
        [query_value_bias.reshape(2 * LAYERS, head_cols), hidden_bias.reshape(-1, head_cols)], axis=0
    )
    bias_all = lax.all_gather(bias_rows, "tensor", axis=0, tiled=False)
    qv_bias = bias_all[:, : 2 * LAYERS].reshape(2, LAYERS, 2, head_cols)
    qv_bias = qv_bias.transpose(1, 2, 0, 3).reshape(LAYERS, 2, 2 * head_cols)
    hidden_full = bias_all[:, 2 * LAYERS :].reshape(2, LAYERS, hidden_cols)
    hidden_full = hidden_full.transpose(1, 0, 2).reshape(LAYERS, 2 * hidden_cols)

    position = jnp.arange(half_len, dtype=jnp.int32)
    mine_pos = position + tensor_idx * half_len
    key_pos = jnp.concatenate([mine_pos, position + (1 - tensor_idx) * half_len])
    first_end = doc_lengths[0, 0]
    second_end = first_end + doc_lengths[0, 1]

    def segment(pos):
        return (pos >= first_end).astype(jnp.int32) + (pos >= second_end).astype(jnp.int32)

    same_doc = segment(mine_pos)[:, None] == segment(key_pos)[None, :]

    cut = [0, head_cols, 2 * head_cols, 3 * head_cols, 4 * head_cols, 4 * head_cols + hidden_cols, 4 * head_cols + 2 * hidden_cols]

    def section(layer_idx, which, part):
        return weights[layer_idx][part, :, cut[which] : cut[which + 1]]

    def project(values, layer_idx, which):
        return jnp.concatenate([nn(values, section(layer_idx, which, p)) for p in range(2)], axis=1)

    def project_back(values, layer_idx, which):
        width = values.shape[1] // 2
        return nt(values[:, :width], section(layer_idx, which, 0)) + nt(
            values[:, width:], section(layer_idx, which, 1)
        )

    hidden_state = tokens[0].astype(jnp.float32)
    rounded = tokens[0]
    saved_acts = []
    for layer_idx in range(LAYERS):
        rows = jnp.concatenate([rounded, swap_halves(rounded)], axis=0)
        query_b = (project(rounded, layer_idx, 0) + qv_bias[layer_idx, 0]).astype(jnp.bfloat16)
        key_b = project(rows, layer_idx, 1).astype(jnp.bfloat16)
        value_b = (project(rows, layer_idx, 2) + qv_bias[layer_idx, 1]).astype(jnp.bfloat16)
        query_h, key_h, value_h = split_heads(query_b), split_heads(key_b), split_heads(value_b)
        scores = (
            jnp.einsum("hqd,hkd->hqk", query_h, key_h, preferred_element_type=jnp.float32) * scale_factor
        )
        scores = jnp.where(same_doc[None], scores, masked_value)
        row_max = jnp.max(scores, axis=-1, keepdims=True)
        raised = jnp.exp(scores - row_max)
        row_total = jnp.sum(raised, axis=-1, keepdims=True)
        attn_probs = (raised / row_total).astype(jnp.bfloat16)
        log_total = row_max + jnp.log(row_total)
        attended = jnp.einsum("hqk,hkd->hqd", attn_probs, value_h, preferred_element_type=jnp.float32)
        attended_b = join_heads(attended.astype(jnp.bfloat16))
        branch = project_back(attended_b, layer_idx, 3)
        normed, normal_one, inverse_one = layer_norm(
            hidden_state + branch + shifts[layer_idx, 0], gains[layer_idx, 0], shifts[layer_idx, 1]
        )
        normed_low = normed.astype(jnp.bfloat16)
        pre_act = project(normed_low, layer_idx, 4) + hidden_full[layer_idx]
        activated_b = exact_gelu(pre_act).astype(jnp.bfloat16)
        mlp_out = project_back(activated_b, layer_idx, 5)
        hidden_state, normal_two, inverse_two = layer_norm(
            normed + mlp_out + shifts[layer_idx, 2], gains[layer_idx, 1], shifts[layer_idx, 3]
        )
        saved_acts.append(
            (rows, query_h, key_h, value_h, log_total, attended_b, normal_one, inverse_one, normed_low,
             pre_act, activated_b, normal_two, inverse_two)
        )
        rounded = hidden_state.astype(jnp.bfloat16)
    output = hidden_state

    state_grad = cotangent[0]
    weight_parts = [None] * LAYERS
    small_parts = [None] * LAYERS
    for layer_idx in reversed(range(LAYERS)):
        (rows, query_h, key_h, value_h, log_total, attended_b, normal_one, inverse_one, normed_low,
         pre_act, activated_b, normal_two, inverse_two) = saved_acts[layer_idx]
        pre_two_grad = norm_back(state_grad, normal_two, inverse_two, gains[layer_idx, 1])
        gain_two = jnp.sum(state_grad * normal_two, axis=0)
        beta_two = jnp.sum(state_grad, axis=0)
        shift_two = jnp.sum(pre_two_grad, axis=0)
        mlp_grad_b = pre_two_grad.astype(jnp.bfloat16)
        down_local = tn(mlp_grad_b, activated_b).astype(jnp.bfloat16)
        activated_grad = project(mlp_grad_b, layer_idx, 5)
        _, gelu_back = jax.vjp(exact_gelu, pre_act)
        pre_act_grad = gelu_back(activated_grad)[0].astype(jnp.bfloat16)
        hidden_part = jnp.sum(pre_act_grad.astype(jnp.float32), axis=0)
        inner_local = tn(normed_low, pre_act_grad).astype(jnp.bfloat16)
        normed_grad = pre_two_grad + project_back(pre_act_grad, layer_idx, 4)
        pre_one_grad = norm_back(normed_grad, normal_one, inverse_one, gains[layer_idx, 0])
        gain_one = jnp.sum(normed_grad * normal_one, axis=0)
        beta_one = jnp.sum(normed_grad, axis=0)
        shift_one = jnp.sum(pre_one_grad, axis=0)
        attn_grad_b = pre_one_grad.astype(jnp.bfloat16)
        out_local = tn(attn_grad_b, attended_b).astype(jnp.bfloat16)
        attended_grad = project(attn_grad_b, layer_idx, 3).astype(jnp.bfloat16)
        attended_grad_h = split_heads(attended_grad)
        scores = (
            jnp.einsum("hqd,hkd->hqk", query_h, key_h, preferred_element_type=jnp.float32) * scale_factor
        )
        scores = jnp.where(same_doc[None], scores, masked_value)
        probs_full = jnp.exp(scores - log_total)
        probs_low = probs_full.astype(jnp.bfloat16)
        value_grad = jnp.einsum("hqk,hqd->hkd", probs_low, attended_grad_h, preferred_element_type=jnp.float32)
        prob_grad = jnp.einsum("hqd,hkd->hqk", attended_grad_h, value_h, preferred_element_type=jnp.float32)
        row_dot = jnp.sum(prob_grad * probs_full, axis=-1, keepdims=True)
        score_grad = (probs_full * (prob_grad - row_dot)).astype(jnp.bfloat16)
        query_grad = (
            jnp.einsum("hqk,hkd->hqd", score_grad, key_h, preferred_element_type=jnp.float32) * scale_factor
        )
        key_grad = (
            jnp.einsum("hqk,hqd->hkd", score_grad, query_h, preferred_element_type=jnp.float32) * scale_factor
        )
        query_grad_b = join_heads(query_grad.astype(jnp.bfloat16))
        key_grad_b = join_heads(key_grad.astype(jnp.bfloat16))
        value_grad_b = join_heads(value_grad.astype(jnp.bfloat16))
        qv_part = jnp.concatenate(
            [
                jnp.sum(query_grad_b.astype(jnp.float32), axis=0),
                jnp.sum(value_grad_b.astype(jnp.float32), axis=0),
            ]
        )
        query_local = tn(rows[:half_len], query_grad_b).astype(jnp.bfloat16)
        key_local = tn(rows, key_grad_b).astype(jnp.bfloat16)
        value_local = tn(rows, value_grad_b).astype(jnp.bfloat16)
        both = project_back(key_grad_b, layer_idx, 1) + project_back(value_grad_b, layer_idx, 2)
        theirs = swap_halves(both[half_len:].astype(jnp.bfloat16))
        state_grad = (
            pre_one_grad
            + project_back(query_grad_b, layer_idx, 0)
            + both[:half_len]
            + theirs.astype(jnp.float32)
        )
        weight_parts[layer_idx] = (query_local, key_local, value_local, out_local, inner_local, down_local)
        small_parts[layer_idx] = jnp.concatenate(
            [shift_one, beta_one, shift_two, beta_two, gain_one, gain_two, qv_part, hidden_part]
        )
    small = jnp.stack(small_parts).reshape(-1, 2 * hidden_cols).astype(jnp.bfloat16)
    small_rows = small.shape[0]
    small = jnp.pad(small, ((0, -small_rows % 16), (0, 0)))
    with_small = jnp.concatenate([weight_parts[0][5], small], axis=0)
    summed = lax.optimization_barrier(lax.psum((*weight_parts[0][:5], with_small, *weight_parts[1]), ALL))
    small_sum = summed[5][features : features + small_rows].astype(jnp.float32).reshape(LAYERS, -1)
    shift_total = small_sum[:, : 4 * features].reshape(LAYERS, 4, features)
    gain_total = small_sum[:, 4 * features : 6 * features].reshape(LAYERS, 2, features)
    qv_total = lax.dynamic_slice_in_dim(
        small_sum[:, 6 * features : 8 * features].reshape(LAYERS, 2, features), tensor_idx * head_cols, head_cols, 2
    )
    hidden_total = lax.dynamic_slice_in_dim(small_sum[:, 8 * features :], tensor_idx * hidden_cols, hidden_cols, 1)

    def own(layer_idx, which):
        array = summed[6 * layer_idx + which]
        width = array.shape[1] // 2
        part = lax.dynamic_slice(array, (dp_idx * thin, tensor_idx * width), (thin, width))
        return part.astype(jnp.float32).T

    qkv_result = jnp.stack([jnp.stack([own(l, w) for w in range(3)]) for l in range(LAYERS)])
    out_result, inner_result, down_result = (
        jnp.stack([own(l, w) for l in range(LAYERS)]) for w in (3, 4, 5)
    )
    return (
        output[None],
        state_grad[None],
        qkv_result,
        out_result,
        inner_result,
        down_result,
        qv_total,
        hidden_total,
        shift_total,
        gain_total,
    )


def solution(mesh):
    in_specs = (
        P("dp", "tensor", None),
        P("dp", None),
        P(None, None, "tensor", "dp"),
        P(None, "tensor", "dp"),
        P(None, "tensor", "dp"),
        P(None, "tensor", "dp"),
        P(None, None, "tensor"),
        P(None, "tensor"),
        P(),
        P(),
        P("dp", "tensor", None),
    )
    out_specs = (
        P("dp", "tensor", None),
        P("dp", "tensor", None),
        P(None, None, "tensor", "dp"),
        P(None, "tensor", "dp"),
        P(None, "tensor", "dp"),
        P(None, "tensor", "dp"),
        P(None, None, "tensor"),
        P(None, "tensor"),
        P(),
        P(),
    )
    return jax.shard_map(body, mesh=mesh, in_specs=in_specs, out_specs=out_specs, check_vma=False)
```

time: 2030 us -> 779 us (0.38)
  blocking collectives: 826 us -> 7.77 us
  starting transfers between devices: 334 us -> 7.9 us
  waiting for transfers between devices: 454 us -> 322 us
  local copies, waits for them, and re-layouts: 236 us -> 260 us
    psum x2 -> x0, blocking collectives: 339 us -> none  [the longest x1 269 us: body(): lax.psum((jnp.stack(qv_parts), jnp.stack(hidden_parts)), 'dp')]
    unnamed x128 -> x0, starting transfers between devices: 333 us -> none
    all_gather x6 -> x1, waiting for transfers between devices: 364 us -> 77.7 us  [gather_weights(): whole = lax.all_gather(piece, ALL, axis=0, tiled=True)]
    all_gather x10 -> x1, blocking collectives: 275 us -> 7.77 us  [body(): bias_all = lax.all_gather(bias_rows, 'tensor', axis=0, tiled=False)]
    psum x0 -> x1, waiting for transfers between devices: none -> 229 us  [body(): lax.psum((*weight_parts[0][:5], with_small, *weight_parts[1]), ALL)]
    unnamed x1 -> x0, blocking collectives: 213 us -> none
    unnamed x486 -> x277, local copies, waits for them, and re-layouts: 161 us -> 20 us
    slice x11 -> x16, local copies, waits for them, and re-layouts: 7.75 us -> 118 us  [the longest x3 66.7 us: gather_weights(): return [whole[:, :, layer].reshape(2, -1, width) for layer in range(layers)]]
  transfers between devices with their start and end apart: 142 -> 6, of which waited for: 11 -> 4; matrix products, arithmetic and copies ran while one was open for 14% -> 32% of each run, Pallas kernels for 0% -> 0%
where the time goes in v1:
time: 779 us; the launch traced here: 767 us
  waiting for transfers between devices  322 us (41%)
  local copies, waits for them, and re-layouts  260 us (33%)
  matrix products  109 us (14%)
  other arithmetic  41.9 us (5%)
  between operations  18.1 us (2%)
  starting transfers between devices  7.9 us (1%)
    psum x1, waiting for transfers between devices, body(): lax.psum((*weight_parts[0][:5], with_small, *weight_parts[1]), ALL)  229 us
    all_gather x1, waiting for transfers between devices, gather_weights(): whole = lax.all_gather(piece, ALL, axis=0, tiled=True)  77.7 us
    slice x3, local copies, waits for them, and re-layouts, gather_weights(): return [whole[:, :, layer].reshape(2, -1, width) for layer in range(layers)]  66.7 us
    dot_general x14, local copies, waits for them, and re-layouts, nn(): lax.dot_general(left, right, (((1,), (0,)), ((), ())), preferred_element_...  56.9 us
    slice x4, local copies, waits for them, and re-layouts, section(): return weights[layer_idx][part, :, cut[which]:cut[which + 1]]  48.6 us
    reshape x1, local copies, waits for them, and re-layouts, gather_weights(): whole = whole.reshape(2, -1, layers, thin, width)  37.9 us
    dot_general x12, matrix products, tn(): lax.dot_general(left, right, (((0,), (0,)), ((), ())), preferred_element_...  32.4 us
    dot_general x24, matrix products, nt(): lax.dot_general(left, right, (((1,), (1,)), ((), ())), preferred_element_...  30.9 us
  transfers between devices with their start and end apart: 6, of which 4 were waited for; matrix products, arithmetic and copies ran while one was open for 32% of the time, Pallas kernels for 0%

profile of v1, /device:TPU:1, one launch (start us, length us, event | category | flops | bytes accessed | tf_op | source)
XLA Modules:
  0.0 767.2 jit_solution(498150254002817466)
XLA Ops:
  10.1 3.7 collective-permute-start
  15.2 7.8 %all-gather.1 = f32[2,12,384]{2,1,0:T(8,128)S(1)} all-gather(f32[1,12,384]{2,1,0:T(8,128)S(1)} %maximum_bitcast_fusion.15), channel_id=2, replica_groups=mesh['dp'=64,'tensor'=2] {'tensor'}, dimensions={0}, use_global_device_ids=true | all-gather | bytes 55296 | tf_op jit(solution)/shard_map/all_gather | solution.py:98
  35.8 77.7 %all-gather.4.cloned.1.call-done = bf16[3072,4608]{1,0:T(8,128)(2,1)} async-done(((bf16[24,4608]{1,0:T(8,128)(2,1)}), bf16[3072,4608]{1,0:T(8,128)(2,1)}) %all-gather.4.cloned.1.call-update) | async-done | bytes 28311568 | tf_op jit(solution)/shard_map/all_gather | solution.py:60
  113.5 37.9 %reshape.337 = bf16[2,64,2,12,4608]{4,3,2,1,0:T(8,128)(2,1)} reshape(bf16[3072,4608]{1,0:T(8,128)(2,1)} %all-gather.4.cloned.1.call-done) | data formatting | bytes 56623104 | tf_op jit(solution)/shard_map/reshape | solution.py:61
  151.3 25.2 %fusion.282 = (bf16[2,64,1,12,4608]{4,3,2,1,0:T(8,128)(2,1)}, bf16[2,64,1,12,4608]{4,3,2,1,0:T(8,128)(2,1)}) fusion(bf16[2,64,2,12,4608]{4,3,2,1,0:T(8,128)(2,1)} %reshape.337), kind=kLoop, calls=%fused_computation.424 | loop fusion | bytes 56623104 | tf_op jit(solution)/shard_map/slice | solution.py:62
  176.6 20.7 %copy.114 = bf16[2,64,1,12,4608]{4,0,3,1,2:T(2,128)(2,1)S(1)} copy(bf16[2,64,1,12,4608]{4,3,2,1,0:T(8,128)(2,1)} %get-tuple-element.143) | data formatting | bytes 28311552 | tf_op jit(solution)/shard_map/slice | solution.py:62
  197.3 8.5 %fusion.286 = (bf16[1,768,384]{2,0,1:T(2,128)(2,1)}, bf16[1,768,384]{2,0,1:T(2,128)(2,1)}, bf16[1,768,384]{2,0,1:T(2,128)(2,1)S(1)}, bf16[1,768,384]{2,0,1:T(2,1...) fusion(bf16[2,768,4608]{2,0,1:T(2,128)(2,1)S(1)} %bitcast.448), kind=kLoop, calls=%fused_computation.428 | loop fusion | bytes 9437184 | tf_op jit(solution)/shard_map/slice | solution.py:118
  205.8 16.1 %fusion.285 = (bf16[1,768,1536]{2,0,1:T(2,128)(2,1)}, bf16[1,768,1536]{2,0,1:T(2,128)(2,1)}, bf16[1,768,1536]{2,0,1:T(2,128)(2,1)}, bf16[1,768,1536]{2,0,1:T(2,128)(2,1)}) fusion(bf16[2,768,4608]{2,0,1:T(2,128)(2,1)S(1)} %bitcast.449), kind=kLoop, calls=%fused_computation.427 | loop fusion | bytes 18874368 | tf_op jit(solution)/shard_map/slice | solution.py:118
  221.8 20.7 %copy.120 = bf16[2,64,1,12,4608]{4,0,3,1,2:T(2,128)(2,1)S(1)} copy(bf16[2,64,1,12,4608]{4,3,2,1,0:T(8,128)(2,1)} %get-tuple-element.144) | data formatting | bytes 28311552 | tf_op jit(solution)/shard_map/slice | solution.py:62
  242.6 8.0 %fusion.284 = (bf16[1,768,384]{2,0,1:T(2,128)(2,1)}, bf16[1,768,384]{2,0,1:T(2,128)(2,1)}, bf16[1,768,384]{2,0,1:T(2,128)(2,1)}, bf16[1,768,384]{2,0,1:T(2,128)(...) fusion(bf16[2,768,4608]{2,0,1:T(2,128)(2,1)S(1)} %bitcast.450), kind=kLoop, calls=%fused_computation.426 | loop fusion | bytes 9437184 | tf_op jit(solution)/shard_map/slice | solution.py:118
  250.5 16.1 %fusion.283 = (bf16[1,768,1536]{2,0,1:T(2,128)(2,1)}, bf16[1,768,1536]{2,0,1:T(2,128)(2,1)}, bf16[1,768,1536]{2,0,1:T(2,128)(2,1)}, bf16[1,768,1536]{2,0,1:T(2,128)(2,1)}) fusion(bf16[2,768,4608]{2,0,1:T(2,128)(2,1)S(1)} %bitcast.451), kind=kLoop, calls=%fused_computation.425 | loop fusion | bytes 18874368 | tf_op jit(solution)/shard_map/slice | solution.py:118
  266.6 4.5 copy.175
  271.2 4.5 copy.174
  278.7 4.6 copy.164
  307.5 7.8 %multiply_convert_fusion.3 = (bf16[256,3072]{1,0:T(8,128)(2,1)S(1)}, f32[256,3072]{1,0:T(8,128)}) fusion(f32[256,1536]{1,0:T(8,128)S(1)} %fusion.52, f32[256,1536]{1,0:T(8,128)S(1)} %fusion.56, f32[3072]{0:T(1024)S(1)} %bitcast.528), kind=kLoop, calls=%fused_computation.50 | loop fusion | flops 52690944 | bytes 7876608 | tf_op jit(solution)/shard_map/convert_element_type | solution.py:155
  320.4 4.7 copy.173
  325.1 4.5 copy.172
  329.7 4.5 copy.171
  334.2 4.5 copy.170
  338.7 4.5 copy.169
  343.2 4.5 copy.168
  347.7 3.4 copy.167
  351.5 3.5 copy.166
  371.1 7.2 multiply_convert_fusion.2
  387.7 3.8 convolution_convert_fusion.1
  432.5 3.5 add_add_fusion.1
  442.4 3.5 convolution_convert_fusion
  454.9 3.7 convolution_convert_fusion.3
  458.7 3.5 convolution_convert_fusion.2
  477.2 4.9 fusion.3
  497.1 13.5 %collective-permute-done.3 = bf16[256,768]{1,0:T(8,128)(2,1)} collective-permute-done((bf16[256,768]{1,0:T(8,128)(2,1)}, bf16[256,768]{1,0:T(8,128)(2,1)}, u32[]{:S(2)}, u32[]{:S(2)}) %collective-permute-start.3) | collective-permute-done | bytes 393248 | tf_op jit(solution)/shard_map/ppermute | solution.py:49
  513.4 229.2 %all-reduce.4.cloned.1.call-done = (bf16[768,768]{0,1:T(8,128)(2,1)}, bf16[768,768]{1,0:T(8,128)(2,1)}, bf16[768,768]{1,0:T(8,128)(2,1)}, bf16[768,768]{1,0:T(8,...) async-done(((bf16[768,768]{0,1:T(8,128)(2,1)}, ...) | async-done | bytes 28409872 | tf_op jit(solution)/shard_map/psum | solution.py:237
  (474 shorter events, 178.3 us)
Async XLA Ops:
  7.2 106.3 %all-gather.4.cloned.1.call-start = ((), (), s32[]{:S(2)}) async-start(), calls=%async_computation | async-start | bytes 28532736 | tf_op jit(solution)/shard_map/all_gather | solution.py:60
  10.0 732.6 %all-reduce.4.cloned.1.call-start = ((), (), s32[]{:S(2)}) async-start(), calls=%async_computation.1 | async-start | bytes 56819712 | tf_op jit(solution)/shard_map/psum | solution.py:237
  10.1 281.5 %collective-permute-start = (bf16[256,768]{1,0:T(8,128)(2,1)}, bf16[256,768]{1,0:T(8,128)(2,1)}, u32[]{:S(2)}, u32[]{:S(2)}) collective-permute-start(bf16[256,768]{1,0:T(8,128)(2,1)} %bitcast.466), channel_id=1, source_target_pairs={{0,1},{1,0},{2,3},{3,2},{4,5},{5,4},{6,7},{7,6},{8,9},{9,8},{10,11... | collective-permute-start | bytes 1179656 | tf_op jit(solution)/shard_map/ppermute | solution.py:49
  32.8 283.3 %copy-start.62 = (f32[768]{0:T(1024)}, f32[768]{0:T(1024)S(1)}, u32[]{:S(2)}) copy-start(f32[768]{0:T(1024)S(1)} %get-tuple-element.109) | copy-start | bytes 9220
  35.8 271.6 %copy-start.67 = (f32[1,2,1536]{2,0,1:T(1,128)}, f32[1,2,1536]{2,0,1:T(1,128)S(1)}, u32[]{:S(2)}) copy-start(f32[1,2,1536]{2,0,1:T(1,128)S(1)} %get-tuple-element.175) | copy-start | bytes 36868
  205.8 70.0 %copy-start.2 = (bf16[1,768,384]{2,0,1:T(2,128)(2,1)}, bf16[1,768,384]{2,0,1:T(2,128)(2,1)S(1)}, u32[]{:S(2)}) copy-start(bf16[1,768,384]{2,0,1:T(2,128)(2,1)S(1)} %get-tuple-element.163) | copy-start | bytes 1769476
  205.8 77.5 %copy-start.6 = (bf16[1,768,384]{2,0,1:T(2,128)(2,1)}, bf16[1,768,384]{2,0,1:T(2,128)(2,1)S(1)}, u32[]{:S(2)}) copy-start(bf16[1,768,384]{2,0,1:T(2,128)(2,1)S(1)} %get-tuple-element.165) | copy-start | bytes 1769476
  205.8 80.5 %copy-start.4 = (bf16[1,768,384]{2,0,1:T(2,128)(2,1)}, bf16[1,768,384]{2,0,1:T(2,128)(2,1)S(1)}, u32[]{:S(2)}) copy-start(bf16[1,768,384]{2,0,1:T(2,128)(2,1)S(1)} %get-tuple-element.166) | copy-start | bytes 1769476
  278.7 10.7 %copy-start.22 = (bf16[1,256,768]{2,1,0:T(8,128)(2,1)S(1)}, bf16[1,256,768]{2,1,0:T(8,128)(2,1)}, u32[]{:S(2)}) copy-start(bf16[1,256,768]{2,1,0:T(8,128)(2,1)} %param.11) | copy-start | bytes 1179652
  305.3 10.8 %copy-start.87 = (f32[256]{0:T(256)}, f32[256]{0:T(256)S(1)}, u32[]{:S(2)}) copy-start(f32[256]{0:T(256)S(1)} %broadcast_multiply_fusion.11) | copy-start | bytes 3076
  305.5 10.6 %copy-start.93 = (f32[256]{0:T(256)}, f32[256]{0:T(256)S(1)}, u32[]{:S(2)}) copy-start(f32[256]{0:T(256)S(1)} %add_rsqrt_fusion.3) | copy-start | bytes 3076
  305.6 9.7 %slice-start.6 = ((s8[4718592]{0:T(1024)(128)(4,1)}), s8[4194304]{0:T(1024)(128)(4,1)S(1)}, s32[]{:S(2)}) async-start(s8[4718592]{0:T(1024)(128)(4,1)} %bitcast.458), calls=%async_computation.8 | async-start | bytes 8388608
  306.5 8.7 %copy-start.18 = (f32[256,1536]{1,0:T(8,128)}, f32[256,1536]{1,0:T(8,128)S(1)}, u32[]{:S(2)}) copy-start(f32[256,1536]{1,0:T(8,128)S(1)} %fusion.52) | copy-start | bytes 4718596
  306.5 8.7 %slice-start.7 = ((s8[4718592]{0:T(1024)(128)(4,1)}), s8[524288]{0:T(1024)(128)(4,1)S(1)}, s32[]{:S(2)}) async-start(s8[4718592]{0:T(1024)(128)(4,1)} %bitcast.458), calls=%async_computation.9 | async-start | bytes 1048576
  307.4 7.8 %copy-start.20 = (f32[256,1536]{1,0:T(8,128)}, f32[256,1536]{1,0:T(8,128)S(1)}, u32[]{:S(2)}) copy-start(f32[256,1536]{1,0:T(8,128)S(1)} %fusion.56) | copy-start | bytes 4718596
  307.4 8.7 %slice-start.2 = ((s8[4718592]{0:T(1024)(128)(4,1)}), s8[4194304]{0:T(1024)(128)(4,1)S(1)}, s32[]{:S(2)}) async-start(s8[4718592]{0:T(1024)(128)(4,1)} %bitcast.454), calls=%async_computation.4 | async-start | bytes 8388608
  307.5 8.7 %slice-start.3 = ((s8[4718592]{0:T(1024)(128)(4,1)}), s8[524288]{0:T(1024)(128)(4,1)S(1)}, s32[]{:S(2)}) async-start(s8[4718592]{0:T(1024)(128)(4,1)} %bitcast.454), calls=%async_computation.5 | async-start | bytes 1048576
  317.2 51.0 %copy-start.75 = (f32[256]{0:T(256)}, f32[256]{0:T(256)S(1)}, u32[]{:S(2)}) copy-start(f32[256]{0:T(256)S(1)} %broadcast_multiply_fusion.10) | copy-start | bytes 3076
  317.4 50.8 %copy-start.85 = (f32[256]{0:T(256)}, f32[256]{0:T(256)S(1)}, u32[]{:S(2)}) copy-start(f32[256]{0:T(256)S(1)} %add_rsqrt_fusion.2) | copy-start | bytes 3076
  317.6 37.8 %collective-permute-start.1 = (bf16[256,768]{1,0:T(8,128)(2,1)S(1)}, bf16[256,768]{1,0:T(8,128)(2,1)}, u32[]{:S(2)}, u32[]{:S(2)}) collective-permute-start(bf16[256,768]{1,0:T(8,128)(2,1)S(1)} %fusion.151), channel_id=1, source_target_pairs={{0,1},{1,0},{2,3},{3,2},{4,5},{5,4},{6,7},{7,6},{8,9},{9,8},{10,11... | collective-permute-start | bytes 1179656 | tf_op jit(solution)/shard_map/ppermute | solution.py:49
  351.5 7.3 copy-start.51
  369.1 9.2 %slice-start.12 = ((s8[4718592]{0:T(1024)(128)(4,1)}), s8[4194304]{0:T(1024)(128)(4,1)S(1)}, s32[]{:S(2)}) async-start(s8[4718592]{0:T(1024)(128)(4,1)} %bitcast.464), calls=%async_computation.14 | async-start | bytes 8388608
  370.0 8.3 %slice-start.13 = ((s8[4718592]{0:T(1024)(128)(4,1)}), s8[524288]{0:T(1024)(128)(4,1)S(1)}, s32[]{:S(2)}) async-start(s8[4718592]{0:T(1024)(128)(4,1)} %bitcast.464), calls=%async_computation.15 | async-start | bytes 1048576
  370.9 8.3 %slice-start.10 = ((s8[4718592]{0:T(1024)(128)(4,1)}), s8[4194304]{0:T(1024)(128)(4,1)S(1)}, s32[]{:S(2)}) async-start(s8[4718592]{0:T(1024)(128)(4,1)} %bitcast.462), calls=%async_computation.12 | async-start | bytes 8388608
  371.1 8.1 %slice-start.11 = ((s8[4718592]{0:T(1024)(128)(4,1)}), s8[524288]{0:T(1024)(128)(4,1)S(1)}, s32[]{:S(2)}) async-start(s8[4718592]{0:T(1024)(128)(4,1)} %bitcast.462), calls=%async_computation.13 | async-start | bytes 1048576
  436.1 11.7 %collective-permute-start.2 = (bf16[256,768]{1,0:T(8,128)(2,1)S(1)}, bf16[256,768]{1,0:T(8,128)(2,1)S(1)}, u32[]{:S(2)}, u32[]{:S(2)}) collective-permute-start(bf16[256,768]{1,0:T(8,128)(2,1)S(1)} %slice.496), channel_id=1, source_target_pairs={{0,1},{1,0},{2,3},{3,2},{4,5},{5,4},{6,7},{7,6},{8,9},{9,8},{10,11... | collective-permute-start | bytes 1179656 | tf_op jit(solution)/shard_map/ppermute | solution.py:49
  436.4 12.5 %slice-start.8 = ((s8[4718592]{0:T(1024)(128)(4,1)}), s8[4194304]{0:T(1024)(128)(4,1)S(1)}, s32[]{:S(2)}) async-start(s8[4718592]{0:T(1024)(128)(4,1)} %bitcast.460), calls=%async_computation.10 | async-start | bytes 8388608
  442.4 7.3 slice-start.4
  454.1 8.1 %slice-start.16 = ((s8[4718592]{0:T(1024)(128)(4,1)}), s8[4194304]{0:T(1024)(128)(4,1)S(1)}, s32[]{:S(2)}) async-start(s8[4718592]{0:T(1024)(128)(4,1)} %bitcast.475), calls=%async_computation.18 | async-start | bytes 8388608
  467.7 14.3 %copy-start.30 = (bf16[12,512,64]{1,2,0:T(8,128)(2,1)}, bf16[12,512,64]{1,2,0:T(8,128)(2,1)S(1)}, u32[]{:S(2)}) copy-start(bf16[12,512,64]{1,2,0:T(8,128)(2,1)S(1)} %get-tuple-element.204) | copy-start | bytes 2359300
  473.5 11.4 %copy-start.33 = (bf16[12,512,64]{1,2,0:T(8,128)(2,1)}, bf16[12,512,64]{1,2,0:T(8,128)(2,1)S(1)}, u32[]{:S(2)}) copy-start(bf16[12,512,64]{1,2,0:T(8,128)(2,1)S(1)} %multiply_convert_fusion.4) | copy-start | bytes 2359300
  494.6 16.0 %collective-permute-start.3 = (bf16[256,768]{1,0:T(8,128)(2,1)}, bf16[256,768]{1,0:T(8,128)(2,1)}, u32[]{:S(2)}, u32[]{:S(2)}) collective-permute-start(bf16[256,768]{1,0:T(8,128)(2,1)} %slice.495), channel_id=1, source_target_pairs={{0,1},{1,0},{2,3},{3,2},{4,5},{5,4},{6,7},{7,6},{8,9},{9,8},{10,11... | collective-permute-start | bytes 1179656 | tf_op jit(solution)/shard_map/ppermute | solution.py:49
  (103 other events, 308.3 us)
Sparse Core Ops, SparseCore 0:
  11.7 101.7 all-gather.3
  487.9 254.6 all-reduce.3
